TPU v7x, 256 devices: a whole 4x4x8 slice. The times are simulated.
256 devices in a mesh: seq: 64 (over x, z, y_lo), head: 4 (over y_hi, core).
Axes of the slice: x: 4, y: 4 (y_hi: 2, y_lo: 2; y = y_hi * 2 + y_lo), z: 8, core: 2. Of those that a mesh axis runs over, the one named last changes fastest.
Arguments:
- inputs: bfloat16 [131072, 1024], P('seq'), may hold values from -32 to 32
- latent_array: bfloat16 [2048, 1024], P('seq'), may hold values from -16 to 16
- w_query: bfloat16 [1024, 1024], P(None, 'head'), may hold values from -4 to 4
- w_key: bfloat16 [1024, 1024], P(None, 'head'), may hold values from -4 to 4
- w_value: bfloat16 [1024, 1024], P(None, 'head'), may hold values from -0.1875 to 0.1875
- w_out: bfloat16 [1024, 1024], P('head'), may hold values from -0.1875 to 0.1875
- w_up: bfloat16 [1024, 4096], P(None, 'head'), may hold values from -0.1875 to 0.1875
- w_down: bfloat16 [4096, 1024], P('head'), may hold values from -0.09375 to 0.09375
Outputs:
- latent_out: bfloat16 [2048, 1024], P('seq', 'head')
All inputs are finite; a program needn't handle non-finite values.
Results may differ from a plain program's by a relative error of at most 0.01355.
The roundings to bfloat16 on the way count: a program that leaves them out, or rounds other values in their place, can miss the bound.
Values may be sent and summed in bfloat16 or wider, within the bound.
No kernel may reach another device: no remote copies, remote signals or barrier semaphores. Data moves between devices by JAX's collectives and lax.ppermute only.
A program may use at most 320 MiB of HBM per device.

v0:
```python
import jax
import jax.numpy as jnp
from jax import lax
from jax.sharding import PartitionSpec as P

HEAD_DIM = 64


def shifted(value, axis, by):
    size = lax.axis_size(axis)
    return lax.ppermute(value, axis, [(i, (i + by) % size) for i in range(size)])


def layer_norm(entries):
    widened = entries.astype(jnp.float32)
    width = widened.shape[-1]
    row_mean = jnp.sum(widened, axis=-1, keepdims=True) / width
    row_square = jnp.sum(widened * widened, axis=-1, keepdims=True) / width
    row_var = row_square - row_mean * row_mean
    return (widened - row_mean) * lax.rsqrt(row_var + 1e-05)


def softmax_merge(earlier, later):
    high_one, sum_one, acc_one = earlier
    high_two, sum_two, acc_two = later
    highest = jnp.maximum(high_one, high_two)
    factor_one = jnp.exp(high_one - highest)
    factor_two = jnp.exp(high_two - highest)
    total = factor_one * sum_one + factor_two * sum_two
    count_rows = acc_one.shape[0]
    count_heads = high_one.shape[1]
    accum = factor_one[..., None] * acc_one.reshape(count_rows, count_heads, -1) + factor_two[
        ..., None
    ] * acc_two.reshape(count_rows, count_heads, -1)
    return (highest, total, accum.reshape(count_rows, -1))


def softmax_terms(query_rows, key_heads, value_heads):
    count_rows = query_rows.shape[0]
    count_heads = key_heads.shape[1]
    query_heads = query_rows.reshape(count_rows, count_heads, -1)
    scores = jnp.einsum("lhd,thd->lht", query_heads, key_heads, preferred_element_type=jnp.float32)
    shard_max = jnp.max(scores, axis=2)
    weights = jnp.exp(scores - shard_max[..., None]).astype(jnp.bfloat16)
    shard_sum = jnp.sum(weights, axis=2, dtype=jnp.float32)
    shard_acc = jnp.einsum("lht,thd->lhd", weights, value_heads, preferred_element_type=jnp.float32)
    return (shard_max, shard_sum, shard_acc.reshape(count_rows, -1))


def on_device(inputs, latent_array, w_query, w_key, w_value, w_out, w_up, w_down):
    score_scale = HEAD_DIM ** (-0.5)
    heads_here = w_query.shape[1] // HEAD_DIM
    lat_rows = latent_array.shape[0]
    tok_rows = inputs.shape[0]
    inner_here = w_query.shape[1]
    seq_count = lax.axis_size("seq")
    position = lax.axis_index("seq")
    normed_input = layer_norm(inputs).astype(jnp.bfloat16)
    key_heads = jnp.dot(normed_input, w_key, preferred_element_type=jnp.float32).astype(
        jnp.bfloat16
    )
    value_heads = jnp.dot(normed_input, w_value, preferred_element_type=jnp.float32).astype(
        jnp.bfloat16
    )
    key_heads = key_heads.reshape(tok_rows, heads_here, HEAD_DIM)
    value_heads = value_heads.reshape(tok_rows, heads_here, HEAD_DIM)
    normed_latent = layer_norm(latent_array).astype(jnp.bfloat16)
    queries = (
        jnp.dot(normed_latent, w_query, preferred_element_type=jnp.float32) * score_scale
    ).astype(jnp.bfloat16)
    all_queries = lax.all_gather(queries, "seq", axis=0, tiled=True)
    start_state = (
        jnp.full((lat_rows, heads_here), -1e30, jnp.float32),
        jnp.zeros((lat_rows, heads_here), jnp.float32),
        jnp.zeros((lat_rows, inner_here), jnp.float32),
    )

    def cycle_turn(turn_index, carried):
        owner = (position - turn_index) % seq_count
        query_part = lax.dynamic_slice_in_dim(all_queries, owner * lat_rows, lat_rows, 0)
        carried = softmax_merge(carried, softmax_terms(query_part, key_heads, value_heads))
        return shifted((carried[0], carried[1], carried[2]), "seq", 1)

    merged = lax.fori_loop(0, seq_count, cycle_turn, start_state)
    highest, total, accum = merged
    attended = (
        (accum.reshape(lat_rows, heads_here, HEAD_DIM) / total[..., None])
        .reshape(lat_rows, inner_here)
        .astype(jnp.bfloat16)
    )
    partial_proj = jnp.dot(attended, w_out, preferred_element_type=jnp.float32)
    width = latent_array.shape[1]
    columns = width // lax.axis_size("head")
    head_place = lax.axis_index("head")
    share = lax.psum_scatter(partial_proj, "head", scatter_dimension=1, tiled=True)
    own_latent = lax.dynamic_slice_in_dim(latent_array, head_place * columns, columns, 1)
    resid_part = (own_latent.astype(jnp.float32) + share).astype(jnp.bfloat16)
    resid_float = resid_part.astype(jnp.float32)
    totals, squares = lax.psum(
        (jnp.sum(resid_float, axis=1), jnp.sum(resid_float * resid_float, axis=1)), "head"
    )
    row_mean = totals / width
    row_var = squares / width - row_mean * row_mean
    normed_part = ((resid_float - row_mean[:, None]) * lax.rsqrt(row_var + 1e-05)[:, None]).astype(
        jnp.bfloat16
    )
    up_proj = jnp.dot(
        lax.all_gather(normed_part, "head", axis=1, tiled=True),
        w_up,
        preferred_element_type=jnp.float32,
    )
    hidden_units = jax.nn.gelu(up_proj, approximate=False).astype(jnp.bfloat16)
    down_share = lax.psum_scatter(
        jnp.dot(hidden_units, w_down, preferred_element_type=jnp.float32).astype(jnp.bfloat16),
        "head",
        scatter_dimension=1,
        tiled=True,
    ).astype(jnp.float32)
    return (resid_part.astype(jnp.float32) + down_share).astype(jnp.bfloat16)


def solution(mesh):
    placed = (
        P("seq", None),
        P("seq", None),
        P(None, "head"),
        P(None, "head"),
        P(None, "head"),
        P("head", None),
        P(None, "head"),
        P("head", None),
    )
    return jax.shard_map(
        on_device, mesh=mesh, in_specs=placed, out_specs=P("seq", "head"), check_vma=False
    )
```

profile of v0, /device:TPU:1, one launch (start us, length us, event | category | flops | bytes accessed | tf_op | source)
XLA Modules:
  0.0 1148.4 jit_solution(16142002720667254548)
XLA Ops:
  18.1 249.1 %all-gather.2.cloned.1.call-done = bf16[2048,256]{1,0:T(8,128)(2,1)} async-done(((bf16[32,256]{1,0:T(8,128)(2,1)}), bf16[2048,256]{1,0:T(8,128)(2,1)}) %all-gather.2.cloned.1.call-update) | async-done | bytes 1048592 | tf_op jit(solution)/shard_map/all_gather | solution.py:71
  267.2 676.8 %while.19 = (s32[]{:T(128)}, f32[32,4]{0,1:T(4,128)S(1)}, f32[32,4]{0,1:T(4,128)S(1)}, f32[32,256]{1,0:T(8,128)S(1)}, s32[]{:T(128)}, /*index=5*/bf16[2048,256]{...) while((s32[]{:T(128)}, f32[32,4]{0,1:T(4,128)S(1)}, ...), condition=%wide.region_7.8_spmd, body=%wide.region_4.7_spmd.sunk | while | flops 68968976 | bytes 5729704 | solution.py:84
  283.0 6.8 collective-permute-done
  293.6 6.8 collective-permute-done
  304.1 6.8 collective-permute-done
  314.7 6.8 collective-permute-done
  325.2 6.8 collective-permute-done
  335.7 6.8 collective-permute-done
  356.8 6.8 collective-permute-done
  367.3 6.8 collective-permute-done
  377.8 6.8 collective-permute-done
  388.3 6.8 collective-permute-done
  398.9 7.2 collective-permute-done
  409.8 6.8 collective-permute-done
  420.3 6.8 collective-permute-done
  441.4 6.8 collective-permute-done
  451.9 6.8 collective-permute-done
  462.4 6.8 collective-permute-done
  473.0 6.8 collective-permute-done
  494.0 6.8 collective-permute-done
  504.6 7.1 collective-permute-done
  515.4 6.8 collective-permute-done
  536.4 6.8 collective-permute-done
  547.0 6.8 collective-permute-done
  557.5 6.8 collective-permute-done
  568.0 6.8 collective-permute-done
  831.2 7.1 collective-permute-done
  936.8 7.3 collective-permute-done
  946.3 143.6 %reduce-scatter.3.cloned.1.call-done = f32[32,256]{1,0:T(8,128)} async-done(((f32[32,1024]{1,0:T(8,128)}), f32[32,256]{1,0:T(8,128)}) %reduce-scatter.3.cloned.1.call-update) | async-done | bytes 32784 | tf_op jit(solution)/shard_map/reduce_scatter | solution.py:95
  1090.8 7.7 all-reduce
  1098.5 7.2 all_gather.7
  1109.1 31.5 %reduce-scatter.5.cloned.1.call-done = bf16[32,256]{1,0:T(8,128)(2,1)} async-done(((bf16[32,1024]{1,0:T(8,128)(2,1)}), bf16[32,256]{1,0:T(8,128)(2,1)}) %reduce-scatter.5.cloned.1.call-update) | async-done | bytes 16400 | tf_op jit(solution)/shard_map/reduce_scatter | solution.py:113
  (968 shorter events, 514.7 us)
Async XLA Ops:
  6.5 260.7 %all-gather.2.cloned.1.call-start = ((), (), s32[]{:S(2)}) async-start(), calls=%async_computation.2 | async-start | bytes 1064960 | tf_op jit(solution)/shard_map/all_gather | solution.py:71
  9.6 1080.3 %reduce-scatter.3.cloned.1.call-start = ((), (), s32[]{:S(2)}) async-start(), calls=%async_computation.3 | async-start | bytes 163840 | tf_op jit(solution)/shard_map/reduce_scatter | solution.py:95
  270.7 8.7 collective-permute-start.2
  282.8 7.1 collective-permute-start.2
  293.4 7.1 collective-permute-start.2
  325.0 7.1 collective-permute-start.2
  335.5 7.1 collective-permute-start.2
  346.0 7.1 collective-permute-start.2
  377.6 7.1 collective-permute-start.2
  388.1 7.1 collective-permute-start.2
  398.6 7.5 collective-permute-start.2
  398.7 7.4 collective-permute-start
  398.8 7.3 collective-permute-start.1
  409.6 7.1 collective-permute-start.2
  420.1 7.1 collective-permute-start.2
  430.6 7.1 collective-permute-start.2
  451.7 7.1 collective-permute-start.2
  462.2 7.1 collective-permute-start.2
  472.7 7.1 collective-permute-start.2
  504.3 7.4 collective-permute-start.2
  504.4 7.3 collective-permute-start
  504.5 7.2 collective-permute-start.1
  525.7 7.1 collective-permute-start.2
  546.7 7.1 collective-permute-start.2
  557.3 7.1 collective-permute-start.2
  830.9 7.4 collective-permute-start.2
  831.0 7.3 collective-permute-start
  831.1 7.3 collective-permute-start.1
  936.5 7.5 collective-permute-start.2
  936.6 7.4 collective-permute-start
  936.7 7.4 collective-permute-start.1
  946.2 194.3 %reduce-scatter.5.cloned.1.call-start = ((), (), s32[]{:S(2)}) async-start(), calls=%async_computation.4 | async-start | bytes 81920 | tf_op jit(solution)/shard_map/reduce_scatter | solution.py:113
  (167 other events, 2243.7 us)
Sparse Core Ops, SparseCore 0:
  9.7 257.4 all-gather.1
  946.4 143.4 reduce-scatter.2
  1109.2 31.2 reduce-scatter.4
where the time goes:
time: 1150 us
  waiting for transfers between devices  863 us (75%)
  matrix products  143 us (12%)
  local copies, waits for them, and re-layouts  67.8 us (6%)
  other arithmetic  28.6 us (2%)
  starting transfers between devices  14.9 us (1%)
  blocking collectives  14.9 us (1%)
  between operations  13.2 us (1%)
    ppermute x192, waiting for transfers between devices, shifted(): lax.ppermute(value, axis, [(i, (i + by) % size) for i in range(size)])  438 us
    all_gather x1, waiting for transfers between devices, on_device(): all_queries = lax.all_gather(queries, 'seq', axis=0, tiled=True)  249 us
    reduce_scatter x1, waiting for transfers between devices, on_device(): lax.psum_scatter(partial_proj, 'head', scatter_dimension=1, tiled=True)  144 us
    dot_general x64, matrix products, softmax_terms(): jnp.einsum('lht,thd->lhd', weights, value_heads, preferred_element_type=j...  109 us
    dynamic_slice x64, local copies, waits for them, and re-layouts, cycle_turn(): lax.dynamic_slice_in_dim(all_queries, owner * lat_rows, lat_rows, 0)  46.1 us
    reduce_scatter x1, waiting for transfers between devices, on_device(): lax.psum_scatter(jnp.dot(hidden_units, w_down, preferred_element_type=jnp...  31.5 us
    dot_general x64, matrix products, softmax_terms(): jnp.einsum('lhd,thd->lht', query_heads, key_heads, preferred_element_type...  23.5 us
  transfers between devices with their start and end apart: 195, of which 68 were waited for; matrix products, arithmetic and copies ran while one was open for 1% of the time, Pallas kernels for 0%

commit v1 on v0

v1 whole, which is shorter than its diff:
```python
import functools

import jax
import jax.numpy as jnp
from jax import lax
from jax.experimental import pallas as pl
from jax.experimental.pallas import tpu as pltpu
from jax.sharding import Mesh
from jax.sharding import PartitionSpec as P

HEAD_DIM = 64
HEADS_HERE = 4
LANES = 128
SEQ = ("x", "z", "ylo")
HEAD = ("yhi", "core")
BF16 = jnp.bfloat16
F32 = jnp.float32
NT = (((1,), (1,)), ((), ()))
NN = (((1,), (0,)), ((), ()))


def product(left, right, numbers=NN):
    return lax.dot_general(left, right, numbers, preferred_element_type=F32)


def params(mib):
    return pltpu.CompilerParams(vmem_limit_bytes=mib * 2**20)


def norm_rows(widened):
    width = widened.shape[-1]
    row_mean = jnp.sum(widened, axis=-1, keepdims=True) / width
    row_square = jnp.sum(widened * widened, axis=-1, keepdims=True) / width
    row_var = row_square - row_mean * row_mean
    return (widened - row_mean) * lax.rsqrt(row_var + 1e-05)


def query_kernel(latent_ref, w_ref, out_ref):
    normed = norm_rows(latent_ref[...].astype(F32)).astype(BF16)
    out_ref[...] = (product(normed, w_ref[...]) * HEAD_DIM ** (-0.5)).astype(BF16)


def make_queries(latent, w_query):
    return pl.pallas_call(
        query_kernel,
        out_shape=jax.ShapeDtypeStruct((latent.shape[0], w_query.shape[1]), BF16),
        compiler_params=params(8),
        name="make_queries",
    )(latent, w_query)


def key_value_kernel(x_ref, w_key_ref, w_value_ref, key_ref, value_ref):
    normed = norm_rows(x_ref[...].astype(F32)).astype(BF16)
    keys = product(normed, w_key_ref[...]).astype(BF16)
    vals = product(normed, w_value_ref[...])
    lane = lax.broadcasted_iota(jnp.int32, (vals.shape[0], LANES), 1)
    low = lane < HEAD_DIM
    for head in range(HEADS_HERE):
        key_ref[head] = keys[:, head * HEAD_DIM : (head + 1) * HEAD_DIM]
        pair = vals[:, head // 2 * LANES : (head // 2 + 1) * LANES]
        one = jnp.where(lane == (HEAD_DIM if head % 2 == 0 else 0), 1.0, 0.0)
        kept = jnp.where(low, pair, one) if head % 2 == 0 else jnp.where(low, one, pair)
        value_ref[head] = kept.astype(BF16)


def make_keys_values(x, w_key, w_value):
    tokens, width = x.shape
    block = 512
    inner = w_key.shape[1]
    return pl.pallas_call(
        key_value_kernel,
        grid=(tokens // block,),
        in_specs=[
            pl.BlockSpec((block, width), lambda i: (i, 0)),
            pl.BlockSpec((width, inner), lambda i: (0, 0)),
            pl.BlockSpec((width, inner), lambda i: (0, 0)),
        ],
        out_specs=[
            pl.BlockSpec((HEADS_HERE, block, HEAD_DIM), lambda i: (0, i, 0)),
            pl.BlockSpec((HEADS_HERE, block, LANES), lambda i: (0, i, 0)),
        ],
        out_shape=[
            jax.ShapeDtypeStruct((HEADS_HERE, tokens, HEAD_DIM), BF16),
            jax.ShapeDtypeStruct((HEADS_HERE, tokens, LANES), BF16),
        ],
        compiler_params=params(24),
        name="make_keys_values",
    )(x, w_key, w_value)


def split_levels(levels, lane):
    first = levels.astype(BF16).astype(F32)
    rest = levels - first
    second = rest.astype(BF16).astype(F32)
    third = rest - second
    parts = jnp.where(lane < 4, first, jnp.where(lane < 8, second, third))
    return jnp.where(lane < 12, parts, 0.0).astype(BF16)


def attend_kernel(count, *refs):
    query_refs, (key_ref, value_ref) = refs[:count], refs[count : count + 2]
    out_refs = refs[count + 2 :]
    rows = query_refs[0].shape[0]
    total_rows = rows * count

    def scores_of(head):
        columns = slice(head * HEAD_DIM, (head + 1) * HEAD_DIM)
        parts = [ref[:, columns] for ref in query_refs]
        part = parts[0] if count == 1 else jnp.concatenate(parts, axis=0)
        return product(part, key_ref[head], NT)

    lane = lax.broadcasted_iota(jnp.int32, (total_rows, LANES), 1)
    levels = jnp.zeros((total_rows, LANES), F32)
    following = scores_of(0)
    even = None
    for head in range(HEADS_HERE):
        scores = following
        if head + 1 < HEADS_HERE:
            following = scores_of(head + 1)
        highest = jnp.max(scores, axis=1, keepdims=True)
        weights = jnp.exp(scores - highest).astype(BF16)
        accum = product(weights, value_ref[head])
        place = HEAD_DIM if head % 2 == 0 else 0
        total = accum[:, place : place + 1]
        mean = accum * (1.0 / total)
        levels = jnp.where(lane % 4 == head, highest + jnp.log(total), levels)
        if head % 2 == 0:
            even = mean
        else:
            both = jnp.where(lane < HEAD_DIM, even, mean).astype(BF16)
            for i, ref in enumerate(out_refs):
                columns = slice(head // 2 * LANES, (head // 2 + 1) * LANES)
                ref[:, columns] = both[i * rows : (i + 1) * rows]
    packed = split_levels(levels, lane)
    for i, ref in enumerate(out_refs):
        ref[:, 2 * LANES :] = packed[i * rows : (i + 1) * rows]


def attend(chunks, keys, values):
    count = len(chunks)
    rows = chunks[0].shape[0]
    return pl.pallas_call(
        functools.partial(attend_kernel, count),
        out_shape=[jax.ShapeDtypeStruct((rows, 3 * LANES), BF16)] * count,
        compiler_params=params(40),
        name="attend",
    )(*chunks, keys, values)


def spread_matrix():
    source = lax.broadcasted_iota(jnp.int32, (LANES, 2 * LANES), 0)
    target = lax.broadcasted_iota(jnp.int32, (LANES, 2 * LANES), 1)
    hit = (source < 12) & (source % 4 == target // HEAD_DIM)
    return jnp.where(hit, 1.0, 0.0).astype(BF16)


def merged(pieces):
    spread = spread_matrix()
    levels = [product(piece[:, 2 * LANES :], spread) for piece in pieces]
    highest = functools.reduce(jnp.maximum, levels)
    total, accum = None, None
    for piece, level in zip(pieces, levels):
        factor = jnp.exp(level - highest)
        term = factor * piece[:, : 2 * LANES].astype(F32)
        total = factor if total is None else total + factor
        accum = term if accum is None else accum + term
    return accum / total, highest, total


def merge_kernel(*refs):
    pieces = [ref[...] for ref in refs[:-1]]
    out_ref = refs[-1]
    mean, highest, total = merged(pieces)
    out_ref[:, : 2 * LANES] = mean.astype(BF16)
    levels = highest + jnp.log(total)
    lane = lax.broadcasted_iota(jnp.int32, (levels.shape[0], LANES), 1)
    one, two = levels[:, :LANES], levels[:, LANES:]
    one_other, two_other = pltpu.roll(one, HEAD_DIM, 1), pltpu.roll(two, HEAD_DIM, 1)
    head = lane % 4
    picked = jnp.where(
        head == 0, one, jnp.where(head == 1, one_other, jnp.where(head == 2, two, two_other))
    )
    out_ref[:, 2 * LANES :] = split_levels(picked, lane)


def merge(pieces):
    return pl.pallas_call(
        merge_kernel,
        out_shape=jax.ShapeDtypeStruct(pieces[0].shape, BF16),
        compiler_params=params(24),
        name="merge",
    )(*pieces)


def finish_kernel(pieces_ref, out_ref):
    mean, highest, total = merged([pieces_ref[i] for i in range(pieces_ref.shape[0])])
    out_ref[...] = mean.astype(BF16)


def finish(pieces):
    return pl.pallas_call(
        finish_kernel,
        out_shape=jax.ShapeDtypeStruct((pieces.shape[1], 2 * LANES), BF16),
        compiler_params=params(8),
        name="finish",
    )(pieces)


def mlp_kernel(att_ref, latent_ref, w_out_ref, w_up_ref, w_down_ref, resid_ref, share_ref):
    count, _, inner = att_ref.shape
    projected = latent_ref[...].astype(F32) + functools.reduce(
        jnp.add,
        [product(att_ref[i], w_out_ref[i * inner : (i + 1) * inner]) for i in range(count)],
    )
    residual = projected.astype(BF16)
    normed = norm_rows(residual.astype(F32)).astype(BF16)
    raised = product(normed, w_up_ref[...])
    hidden = (0.5 * raised * (1.0 + lax.erf(raised * 0.5**0.5))).astype(BF16)
    share = product(hidden, w_down_ref[...]).astype(BF16)
    columns = share.shape[1] // count
    for i in range(count):
        resid_ref[i] = residual[:, i * columns : (i + 1) * columns]
        share_ref[i] = share[:, i * columns : (i + 1) * columns]


def mlp(att, latent, w_out, w_up, w_down):
    count, rows, _ = att.shape
    out = jax.ShapeDtypeStruct((count, rows, latent.shape[1] // count), BF16)
    return pl.pallas_call(
        mlp_kernel,
        out_shape=[out, out],
        compiler_params=params(24),
        name="mlp",
    )(att, latent, w_out, w_up, w_down)


def close_kernel(place_ref, resid_ref, share_ref, out_ref):
    total = functools.reduce(jnp.add, [share_ref[i].astype(F32) for i in range(share_ref.shape[0])])
    out_ref[...] = (resid_ref[place_ref[0]].astype(F32) + total).astype(BF16)


def close(place, resid, shares):
    return pl.pallas_call(
        close_kernel,
        in_specs=[
            pl.BlockSpec(memory_space=pltpu.SMEM),
            pl.BlockSpec(memory_space=pltpu.VMEM),
            pl.BlockSpec(memory_space=pltpu.VMEM),
        ],
        out_shape=jax.ShapeDtypeStruct(resid.shape[1:], BF16),
        compiler_params=params(8),
        name="close",
    )(place, resid, shares)


def moved(value, by_x, by_y):
    size_x, size_y = lax.axis_size("x"), lax.axis_size("ylo")
    pairs = []
    for x in range(size_x):
        for y in range(size_y):
            target = (x + by_x) % size_x * size_y + (y + by_y) % size_y
            pairs.append((x * size_y + y, target))
    return lax.ppermute(value, ("x", "ylo"), pairs)


def along(value, axis, by):
    size = lax.axis_size(axis)
    return lax.ppermute(value, axis, [(i, (i + by) % size) for i in range(size)])


def on_device(inputs, latent, w_query, w_key, w_value, w_out, w_up, w_down):
    rows = latent.shape[0]
    size_z = lax.axis_size("z")
    w_out_all = lax.all_gather(w_out, HEAD, axis=0, tiled=True)
    queries = make_queries(latent, w_query)
    wide = jnp.broadcast_to(queries[None], (size_z,) + queries.shape)
    column = lax.all_to_all(wide, "z", 0, 0, tiled=True).reshape(size_z * rows, -1)
    keys, values = make_keys_values(inputs, w_key, w_value)
    shifts = [(1, 0), (3, 0), (2, 0), (2, 1), (1, 1), (3, 1), (0, 1)]
    arrived = {shift: moved(column, *shift) for shift in shifts}
    pieces = []
    groups = [[None], shifts[0:2], shifts[2:4], shifts[4:6], shifts[6:7]]
    for group in groups:
        chunks = [column if shift is None else arrived[shift] for shift in group]
        outs = attend(chunks, keys, values)
        for shift, out in zip(group, outs):
            if shift is not None:
                out = moved(out, -shift[0], -shift[1])
            pieces.append(out)
    block = merge(pieces)
    parts = lax.all_to_all(block.reshape(size_z, rows, -1), "z", 0, 0, tiled=True)
    attended = finish(parts)
    att = lax.all_gather(attended, HEAD, axis=0)
    resid, shares = mlp(att, latent, w_out_all, w_up, w_down)
    shares = lax.all_to_all(shares, HEAD, 0, 0, tiled=True)
    place = lax.axis_index(HEAD).astype(jnp.int32).reshape(1)
    return close(place, resid, shares)


def solution(mesh):
    fine = Mesh(mesh.devices.reshape(4, 8, 2, 2, 2), SEQ + HEAD)
    placed = (
        P(SEQ, None),
        P(SEQ, None),
        P(None, HEAD),
        P(None, HEAD),
        P(None, HEAD),
        P(HEAD, None),
        P(None, HEAD),
        P(HEAD, None),
    )
    return jax.shard_map(
        on_device, mesh=fine, in_specs=placed, out_specs=P(SEQ, HEAD), check_vma=False
    )
```

time: 1150 us -> 126 us (0.11)
  waiting for transfers between devices: 863 us -> 7.83 us
  matrix products: 143 us -> 0 us
  local copies, waits for them, and re-layouts: 67.8 us -> 9.34 us
  Pallas kernels: 0 us -> 29.7 us
  other arithmetic: 28.6 us -> 0 us
  blocking collectives: 14.9 us -> 42.1 us
    ppermute x192 -> x14, waiting for transfers between devices: 438 us -> 2.35 us  [moved(): return lax.ppermute(value, ('x', 'ylo'), pairs)]
    all_gather x1, waiting for transfers between devices: 249 us -> 0.01 us  [on_device(): w_out_all = lax.all_gather(w_out, HEAD, axis=0, tiled=True)]
    reduce_scatter x2 -> x0, waiting for transfers between devices: 175 us -> none  [the longest x1 144 us: on_device(): lax.psum_scatter(partial_proj, 'head', scatter_dimension=1, tiled=True)]
    dot_general x133 -> x0, matrix products: 143 us -> none  [the longest x64 109 us: softmax_terms(): jnp.einsum('lht,thd->lhd', weights, value_heads, preferred_element_type=j...]
    dynamic_slice x64 -> x0, local copies, waits for them, and re-layouts: 46.1 us -> none  [cycle_turn(): lax.dynamic_slice_in_dim(all_queries, owner * lat_rows, lat_rows, 0)]
    pallas_call x0 -> x11, Pallas kernels: none -> 29.7 us  [the longest x5 21.4 us: attend(): pl.pallas_call(functools.partial(attend_kernel, count), out_shape=[jax.Sh...]
    all_to_all x0 -> x2, blocking collectives: none -> 27.6 us  [the longest x1 16.6 us: on_device(): lax.all_to_all(wide, 'z', 0, 0, tiled=True).reshape(size_z * rows, -1)]
    reduce_sum x67 -> x0, other arithmetic: 25.3 us -> none  [the longest x64 19.7 us: softmax_terms(): shard_sum = jnp.sum(weights, axis=2, dtype=jnp.float32)]
  transfers between devices with their start and end apart: 195 -> 16, of which waited for: 68 -> 2; matrix products, arithmetic and copies ran while one was open for 1% -> 0% of each run, Pallas kernels for 0% -> 22%
where the time goes in v1:
time: 126 us
  blocking collectives  42.1 us (33%)
  Pallas kernels  29.7 us (24%)
  starting transfers between devices  23.2 us (18%)
  between operations  13.6 us (11%)
  local copies, waits for them, and re-layouts  9.34 us (7%)
  waiting for transfers between devices  7.83 us (6%)
    pallas_call x5, Pallas kernels, attend(): pl.pallas_call(functools.partial(attend_kernel, count), out_shape=[jax.Sh...  21.4 us
    ppermute x14, starting transfers between devices, moved(): return lax.ppermute(value, ('x', 'ylo'), pairs)  18.9 us
    all_to_all x1, blocking collectives, on_device(): lax.all_to_all(wide, 'z', 0, 0, tiled=True).reshape(size_z * rows, -1)  16.6 us
    all_gather x1, blocking collectives, on_device(): att = lax.all_gather(attended, HEAD, axis=0)  14.5 us
    all_to_all x1, blocking collectives, on_device(): lax.all_to_all(block.reshape(size_z, rows, -1), 'z', 0, 0, tiled=True)  11 us
    unnamed x18, local copies, waits for them, and re-layouts  9.33 us
    all_to_all x1, waiting for transfers between devices, on_device(): shares = lax.all_to_all(shares, HEAD, 0, 0, tiled=True)  4.76 us
    all_to_all x1, starting transfers between devices, on_device(): shares = lax.all_to_all(shares, HEAD, 0, 0, tiled=True)  4.35 us
  transfers between devices with their start and end apart: 16, of which 2 were waited for; matrix products, arithmetic and copies ran while one was open for 0% of the time, Pallas kernels for 22%

profile of v1, /device:TPU:1, one launch (start us, length us, event | category | flops | bytes accessed | tf_op | source)
XLA Modules:
  0.0 125.8 jit_solution(4533665035382574040)
XLA Ops:
  6.5 0.7 all-gather.3.cloned.1.call-update
  7.3 1.0 copy-done.6
  8.3 0.8 copy-done.7
  9.4 16.6 %all_to_all.15 = bf16[8,32,256]{2,1,0:T(8,128)(2,1)S(1)} all-to-all(bf16[8,32,256]{2,1,0:T(8,128)(2,1)S(1)} %broadcast_in_dim.2), channel_id=1, replica_groups=mesh['x'=4,'z'=8,'ylo'=2,'yhi'=2,'core'=2] {'z'}, dimensions={0} | all-to-all | bytes 262144 | tf_op jit(solution)/shard_map/all_to_all | solution.py:277
  26.0 2.2 %collective-permute-start.8 = (bf16[256,256]{1,0:T(8,128)(2,1)S(1)}, bf16[256,256]{1,0:T(8,128)(2,1)S(1)}, u32[]{:S(2)}, u32[]{:S(2)}) collective-permute-start(bf16[256,256]{1,0:T(8,128)(2,1)S(1)} %bitcast.5), channel_id=1, source_target_pairs={{0,68},{4,64},{64,132},{68,128},{128,196},{132,192},{192,4},{196,0... | collective-permute-start | bytes 393224 | tf_op jit(solution)/shard_map/ppermute | solution.py:263
  28.2 1.4 %collective-permute-start.9 = (bf16[256,256]{1,0:T(8,128)(2,1)S(1)}, bf16[256,256]{1,0:T(8,128)(2,1)S(1)}, u32[]{:S(2)}, u32[]{:S(2)}) collective-permute-start(bf16[256,256]{1,0:T(8,128)(2,1)S(1)} %bitcast.6), channel_id=1, source_target_pairs={{0,196},{4,192},{64,4},{68,0},{128,68},{132,64},{192,132},{196,128... | collective-permute-start | bytes 393224 | tf_op jit(solution)/shard_map/ppermute | solution.py:263
  29.6 1.5 %collective-permute-start.4 = (bf16[256,256]{1,0:T(8,128)(2,1)S(1)}, bf16[256,256]{1,0:T(8,128)(2,1)S(1)}, u32[]{:S(2)}, u32[]{:S(2)}) collective-permute-start(bf16[256,256]{1,0:T(8,128)(2,1)S(1)} %bitcast.7), channel_id=1, source_target_pairs={{0,128},{4,132},{64,192},{68,196},{128,0},{132,4},{192,64},{196,68... | collective-permute-start | bytes 393224 | tf_op jit(solution)/shard_map/ppermute | solution.py:263
  31.1 2.4 %collective-permute-start.5 = (bf16[256,256]{1,0:T(8,128)(2,1)S(1)}, bf16[256,256]{1,0:T(8,128)(2,1)S(1)}, u32[]{:S(2)}, u32[]{:S(2)}) collective-permute-start(bf16[256,256]{1,0:T(8,128)(2,1)S(1)} %bitcast.8), channel_id=1, source_target_pairs={{0,132},{4,128},{64,196},{68,192},{128,4},{132,0},{192,68},{196,64... | collective-permute-start | bytes 393224 | tf_op jit(solution)/shard_map/ppermute | solution.py:263
  33.6 2.2 %copy-done = bf16[2048,1024]{1,0:T(8,128)(2,1)S(1)} copy-done((bf16[2048,1024]{1,0:T(8,128)(2,1)S(1)}, bf16[2048,1024]{1,0:T(8,128)(2,1)}, u32[]{:S(2)}) %copy-start) | copy-done | bytes 4194328
  35.7 1.0 copy-done.4
  36.8 1.0 copy-done.5
  37.8 4.2 %make_keys_values.1 = (bf16[4,2048,64]{2,1,0:T(8,128)(2,1)S(1)}, bf16[4,2048,128]{2,1,0:T(8,128)(2,1)S(1)}) custom-call(bf16[2048,1024]{1,0:T(8,128)(2,1)S(1)} %copy-done, bf16[1024,256]{1,0:T(8,128)(2,1)S(1)} %copy-done.4, bf16[1024,256]{1,0:T(8,128)(2,1)S(1)} %copy-done.5), custom_call_target="tpu_custom_call" | custom-call | tf_op jit(solution)/shard_map/make_keys_values/pallas_call | solution.py:70
  42.1 5.2 %attend.8 = (bf16[256,384]{1,0:T(8,128)(2,1)S(1)}, bf16[256,384]{1,0:T(8,128)(2,1)S(1)}) custom-call(bf16[256,256]{1,0:T(8,128)(2,1)S(1)} %collective-permute-done.8.refs_0_, bf16[256,256]{1,0:T(8,128)(2,1)S(1)} %collective-permute-done.9.refs_1_, bf16[4,2048,64]{2,1,0:T(8,128)(2,1)S(1)} %get-tuple-element.15.refs_1_.refs_2_, ...), custom_call_target="tpu_custom_call" | custom-call | tf_op jit(solution)/shard_map/attend/pallas_call | solution.py:142
  47.4 1.2 collective-permute-start.10
  48.6 1.2 collective-permute-start.11
  49.8 2.7 %collective-permute-start.1 = (bf16[256,256]{1,0:T(8,128)(2,1)S(1)}, bf16[256,256]{1,0:T(8,128)(2,1)S(1)}, u32[]{:S(2)}, u32[]{:S(2)}) collective-permute-start(bf16[256,256]{1,0:T(8,128)(2,1)S(1)} %bitcast.10), channel_id=1, source_target_pairs={{0,192},{4,196},{64,0},{68,4},{128,64},{132,68},{192,128},{196,132... | collective-permute-start | bytes 393224 | tf_op jit(solution)/shard_map/ppermute | solution.py:263
  52.7 5.2 %attend.7 = (bf16[256,384]{1,0:T(8,128)(2,1)S(1)}, bf16[256,384]{1,0:T(8,128)(2,1)S(1)}) custom-call(bf16[256,256]{1,0:T(8,128)(2,1)S(1)} %collective-permute-done.4.refs_0_, bf16[256,256]{1,0:T(8,128)(2,1)S(1)} %collective-permute-done.5.refs_1_, bf16[4,2048,64]{2,1,0:T(8,128)(2,1)S(1)} %get-tuple-element.15.refs_1_.refs_2_, ...), custom_call_target="tpu_custom_call" | custom-call | tf_op jit(solution)/shard_map/attend/pallas_call | solution.py:142
  57.9 1.2 collective-permute-start.6
  59.1 2.9 %collective-permute-start.7 = (bf16[256,384]{1,0:T(8,128)(2,1)S(1)}, bf16[256,384]{1,0:T(8,128)(2,1)S(1)}, u32[]{:S(2)}, u32[]{:S(2)}) collective-permute-start(bf16[256,384]{1,0:T(8,128)(2,1)S(1)} %get-tuple-element.20), channel_id=1, source_target_pairs={{0,132},{4,128},{64,196},{68,192},{128,4},{132,0},{192,68},{196,64... | collective-permute-start | bytes 589832 | tf_op jit(solution)/shard_map/ppermute | solution.py:263
  62.0 5.2 %attend.6 = (bf16[256,384]{1,0:T(8,128)(2,1)S(1)}, bf16[256,384]{1,0:T(8,128)(2,1)S(1)}) custom-call(bf16[256,256]{1,0:T(8,128)(2,1)S(1)} %collective-permute-done.refs_0_, bf16[256,256]{1,0:T(8,128)(2,1)S(1)} %collective-permute-done.1.refs_1_, bf16[4,2048,64]{2,1,0:T(8,128)(2,1)S(1)} %get-tuple-element.15.refs_1_.refs_2_, ...), custom_call_target="tpu_custom_call" | custom-call | tf_op jit(solution)/shard_map/attend/pallas_call | solution.py:142
  67.3 1.3 %collective-permute-start.2 = (bf16[256,384]{1,0:T(8,128)(2,1)S(1)}, bf16[256,384]{1,0:T(8,128)(2,1)S(1)}, u32[]{:S(2)}, u32[]{:S(2)}) collective-permute-start(bf16[256,384]{1,0:T(8,128)(2,1)S(1)} %get-tuple-element.17), channel_id=1, source_target_pairs={{0,192},{4,196},{64,0},{68,4},{128,64},{132,68},{192,128},{196,132... | collective-permute-start | bytes 589832 | tf_op jit(solution)/shard_map/ppermute | solution.py:263
  68.6 2.8 %attend.9 = bf16[256,384]{1,0:T(8,128)(2,1)S(1)} custom-call(bf16[256,256]{1,0:T(8,128)(2,1)S(1)} %collective-permute-done.12.refs_0_, bf16[4,2048,64]{2,1,0:T(8,128)(2,1)S(1)} %get-tuple-element.15.refs_1_.refs_2_, bf16[4,2048,128]{2,1,0:T(8,128)(2,1)S(1)} %get-tuple-element.16.refs_2_.refs_3_), custom_call_target="tpu_custom_call" | custom-call | tf_op jit(solution)/shard_map/attend/pallas_call | solution.py:142
  72.1 2.8 %attend.5.refs_0_ = bf16[256,384]{1,0:T(8,128)(2,1)S(1)} custom-call(bf16[256,256]{1,0:T(8,128)(2,1)S(1)} %bitcast.12, bf16[4,2048,64]{2,1,0:T(8,128)(2,1)S(1)} %get-tuple-element.15.refs_1_.refs_2_, bf16[4,2048,128]{2,1,0:T(8,128)(2,1)S(1)} %get-tuple-element.16.refs_2_.refs_3_), custom_call_target="tpu_custom_call" | custom-call | tf_op jit(solution)/shard_map/attend/pallas_call | solution.py:142
  74.9 2.3 %collective-permute-done.3.refs_2_ = bf16[256,384]{1,0:T(8,128)(2,1)S(1)} collective-permute-done((bf16[256,384]{1,0:T(8,128)(2,1)S(1)}, bf16[256,384]{1,0:T(8,128)(2,1)S(1)}, u32[]{:S(2)}, u32[]{:S(2)}) %collective-permute-start.3) | collective-permute-done | bytes 196640 | tf_op jit(solution)/shard_map/ppermute | solution.py:263
  77.3 1.0 merge.1
  78.2 11.0 %all_to_all.16.pieces_ref = bf16[8,32,384]{2,1,0:T(8,128)(2,1)S(1)} all-to-all(bf16[8,32,384]{2,1,0:T(8,128)(2,1)S(1)} %bitcast.4), channel_id=1, replica_groups=mesh['x'=4,'z'=8,'ylo'=2,'yhi'=2,'core'=2] {'z'}, dimensions={0} | all-to-all | bytes 393216 | tf_op jit(solution)/shard_map/all_to_all | solution.py:291
  89.5 14.5 %all-gather = bf16[128,256]{1,0:T(8,128)(2,1)S(1)} all-gather(bf16[32,256]{1,0:T(8,128)(2,1)S(1)} %finish.1), channel_id=2, replica_groups=mesh['x'=4,'z'=8,'ylo'=2,'yhi'=2,'core'=2] {'yhi','core'}, dimensions={0}, use_global_device_ids=true | all-gather | bytes 81920 | tf_op jit(solution)/shard_map/all_gather | solution.py:293
  104.0 1.6 %copy-done.2 = bf16[1024,1024]{1,0:T(8,128)(2,1)S(1)} copy-done((bf16[1024,1024]{1,0:T(8,128)(2,1)S(1)}, bf16[1024,1024]{1,0:T(8,128)(2,1)}, u32[]{:S(2)}) %copy-start.2) | copy-done | bytes 2097176
  105.6 1.6 %copy-done.3 = bf16[1024,1024]{1,0:T(8,128)(2,1)S(1)} copy-done((bf16[1024,1024]{1,0:T(8,128)(2,1)S(1)}, bf16[1024,1024]{1,0:T(8,128)(2,1)}, u32[]{:S(2)}) %copy-start.3) | copy-done | bytes 2097176
  107.2 2.0 %mlp.1 = (bf16[4,32,256]{2,1,0:T(8,128)(2,1)S(1)}, bf16[4,32,256]{2,1,0:T(8,128)(2,1)}) custom-call(bf16[4,32,256]{2,1,0:T(8,128)(2,1)S(1)} %bitcast.13, bf16[32,1024]{1,0:T(8,128)(2,1)S(1)} %copy-done.8, bf16[1024,1024]{1,0:T(8,128)(2,1)S(1)} %copy-done.3, bf16[1024,1024]{1,0:T(8,128)(2,1)S(1)} %copy-done.1, bf16[1024,1024]{1,0:T(8,128)(2,1)S(1)} %copy-done.2), custom_call_target="tpu_custom_call" | custom-call | tf_op jit(solution)/shard_map/mlp/pallas_call | solution.py:229
  109.2 4.3 %all-to-all-start.2 = ((bf16[4,32,256]{2,1,0:T(8,128)(2,1)}), bf16[4,32,256]{2,1,0:T(8,128)(2,1)S(1)}, u32[]{:S(2)}, u32[]{:S(2)}) async-start(bf16[4,32,256]{2,1,0:T(8,128)(2,1)} %get-tuple-element.24), calls=%async_computation.2 | async-start | bytes 131072 | tf_op jit(solution)/shard_map/all_to_all | solution.py:295
  113.6 4.8 %all-to-all-done.2.share_ref = bf16[4,32,256]{2,1,0:T(8,128)(2,1)S(1)} async-done(((bf16[4,32,256]{2,1,0:T(8,128)(2,1)}), bf16[4,32,256]{2,1,0:T(8,128)(2,1)S(1)}, u32[]{:S(2)}, u32[]{:S(2)}) %all-to-all-start.2) | async-done | bytes 65568 | tf_op jit(solution)/shard_map/all_to_all | solution.py:295
  (34 shorter events, 2.0 us)
Async XLA Ops:
  6.5 97.5 %all-gather.3.cloned.1.call-start = ((), (), s32[]{:S(2)}) async-start(), calls=%async_computation.3 | async-start | bytes 2621440 | tf_op jit(solution)/shard_map/all_gather | solution.py:274
  7.3 1.0 copy-start.6
  8.3 0.8 copy-start.7
  26.0 16.1 %collective-permute-start.8 = (bf16[256,256]{1,0:T(8,128)(2,1)S(1)}, bf16[256,256]{1,0:T(8,128)(2,1)S(1)}, u32[]{:S(2)}, u32[]{:S(2)}) collective-permute-start(bf16[256,256]{1,0:T(8,128)(2,1)S(1)} %bitcast.5), channel_id=1, source_target_pairs={{0,68},{4,64},{64,132},{68,128},{128,196},{132,192},{192,4},{196,0... | collective-permute-start | bytes 393224 | tf_op jit(solution)/shard_map/ppermute | solution.py:263
  28.2 13.9 %collective-permute-start.9 = (bf16[256,256]{1,0:T(8,128)(2,1)S(1)}, bf16[256,256]{1,0:T(8,128)(2,1)S(1)}, u32[]{:S(2)}, u32[]{:S(2)}) collective-permute-start(bf16[256,256]{1,0:T(8,128)(2,1)S(1)} %bitcast.6), channel_id=1, source_target_pairs={{0,196},{4,192},{64,4},{68,0},{128,68},{132,64},{192,132},{196,128... | collective-permute-start | bytes 393224 | tf_op jit(solution)/shard_map/ppermute | solution.py:263
  29.6 20.2 %collective-permute-start.4 = (bf16[256,256]{1,0:T(8,128)(2,1)S(1)}, bf16[256,256]{1,0:T(8,128)(2,1)S(1)}, u32[]{:S(2)}, u32[]{:S(2)}) collective-permute-start(bf16[256,256]{1,0:T(8,128)(2,1)S(1)} %bitcast.7), channel_id=1, source_target_pairs={{0,128},{4,132},{64,192},{68,196},{128,0},{132,4},{192,64},{196,68... | collective-permute-start | bytes 393224 | tf_op jit(solution)/shard_map/ppermute | solution.py:263
  31.1 21.4 %collective-permute-start.5 = (bf16[256,256]{1,0:T(8,128)(2,1)S(1)}, bf16[256,256]{1,0:T(8,128)(2,1)S(1)}, u32[]{:S(2)}, u32[]{:S(2)}) collective-permute-start(bf16[256,256]{1,0:T(8,128)(2,1)S(1)} %bitcast.8), channel_id=1, source_target_pairs={{0,132},{4,128},{64,196},{68,192},{128,4},{132,0},{192,68},{196,64... | collective-permute-start | bytes 393224 | tf_op jit(solution)/shard_map/ppermute | solution.py:263
  33.6 2.2 %copy-start = (bf16[2048,1024]{1,0:T(8,128)(2,1)S(1)}, bf16[2048,1024]{1,0:T(8,128)(2,1)}, u32[]{:S(2)}) copy-start(bf16[2048,1024]{1,0:T(8,128)(2,1)} %x_ref.1) | copy-start | bytes 12582916
  35.7 1.0 copy-start.4
  36.8 1.0 copy-start.5
  47.4 24.1 %collective-permute-start.10 = (bf16[256,384]{1,0:T(8,128)(2,1)S(1)}, bf16[256,384]{1,0:T(8,128)(2,1)S(1)}, u32[]{:S(2)}, u32[]{:S(2)}) collective-permute-start(bf16[256,384]{1,0:T(8,128)(2,1)S(1)} %get-tuple-element.21), channel_id=1, source_target_pairs={{0,196},{4,192},{64,4},{68,0},{128,68},{132,64},{192,132},{196,128... | collective-permute-start | bytes 589832 | tf_op jit(solution)/shard_map/ppermute | solution.py:263
  48.6 23.1 %collective-permute-start.11 = (bf16[256,384]{1,0:T(8,128)(2,1)S(1)}, bf16[256,384]{1,0:T(8,128)(2,1)S(1)}, u32[]{:S(2)}, u32[]{:S(2)}) collective-permute-start(bf16[256,384]{1,0:T(8,128)(2,1)S(1)} %get-tuple-element.22), channel_id=1, source_target_pairs={{0,68},{4,64},{64,132},{68,128},{128,196},{132,192},{192,4},{196,0... | collective-permute-start | bytes 589832 | tf_op jit(solution)/shard_map/ppermute | solution.py:263
  49.8 8.1 %collective-permute-start = (bf16[256,256]{1,0:T(8,128)(2,1)S(1)}, bf16[256,256]{1,0:T(8,128)(2,1)S(1)}, u32[]{:S(2)}, u32[]{:S(2)}) collective-permute-start(bf16[256,256]{1,0:T(8,128)(2,1)S(1)} %bitcast.9), channel_id=1, source_target_pairs={{0,64},{4,68},{64,128},{68,132},{128,192},{132,196},{192,0},{196,4... | collective-permute-start | bytes 393224 | tf_op jit(solution)/shard_map/ppermute | solution.py:263
  49.8 9.3 %collective-permute-start.1 = (bf16[256,256]{1,0:T(8,128)(2,1)S(1)}, bf16[256,256]{1,0:T(8,128)(2,1)S(1)}, u32[]{:S(2)}, u32[]{:S(2)}) collective-permute-start(bf16[256,256]{1,0:T(8,128)(2,1)S(1)} %bitcast.10), channel_id=1, source_target_pairs={{0,192},{4,196},{64,0},{68,4},{128,64},{132,68},{192,128},{196,132... | collective-permute-start | bytes 393224 | tf_op jit(solution)/shard_map/ppermute | solution.py:263
  52.5 14.8 %collective-permute-start.12 = (bf16[256,256]{1,0:T(8,128)(2,1)S(1)}, bf16[256,256]{1,0:T(8,128)(2,1)S(1)}, u32[]{:S(2)}, u32[]{:S(2)}) collective-permute-start(bf16[256,256]{1,0:T(8,128)(2,1)S(1)} %bitcast.11), channel_id=1, source_target_pairs={{0,4},{4,0},{64,68},{68,64},{128,132},{132,128},{192,196},{196,192... | collective-permute-start | bytes 393224 | tf_op jit(solution)/shard_map/ppermute | solution.py:263
  57.9 17.0 %collective-permute-start.6 = (bf16[256,384]{1,0:T(8,128)(2,1)S(1)}, bf16[256,384]{1,0:T(8,128)(2,1)S(1)}, u32[]{:S(2)}, u32[]{:S(2)}) collective-permute-start(bf16[256,384]{1,0:T(8,128)(2,1)S(1)} %get-tuple-element.19), channel_id=1, source_target_pairs={{0,128},{4,132},{64,192},{68,196},{128,0},{132,4},{192,64},{196,68... | collective-permute-start | bytes 589832 | tf_op jit(solution)/shard_map/ppermute | solution.py:263
  59.1 15.8 %collective-permute-start.7 = (bf16[256,384]{1,0:T(8,128)(2,1)S(1)}, bf16[256,384]{1,0:T(8,128)(2,1)S(1)}, u32[]{:S(2)}, u32[]{:S(2)}) collective-permute-start(bf16[256,384]{1,0:T(8,128)(2,1)S(1)} %get-tuple-element.20), channel_id=1, source_target_pairs={{0,132},{4,128},{64,196},{68,192},{128,4},{132,0},{192,68},{196,64... | collective-permute-start | bytes 589832 | tf_op jit(solution)/shard_map/ppermute | solution.py:263
  67.3 7.7 %collective-permute-start.2 = (bf16[256,384]{1,0:T(8,128)(2,1)S(1)}, bf16[256,384]{1,0:T(8,128)(2,1)S(1)}, u32[]{:S(2)}, u32[]{:S(2)}) collective-permute-start(bf16[256,384]{1,0:T(8,128)(2,1)S(1)} %get-tuple-element.17), channel_id=1, source_target_pairs={{0,192},{4,196},{64,0},{68,4},{128,64},{132,68},{192,128},{196,132... | collective-permute-start | bytes 589832 | tf_op jit(solution)/shard_map/ppermute | solution.py:263
  71.4 5.8 %collective-permute-start.3 = (bf16[256,384]{1,0:T(8,128)(2,1)S(1)}, bf16[256,384]{1,0:T(8,128)(2,1)S(1)}, u32[]{:S(2)}, u32[]{:S(2)}) collective-permute-start(bf16[256,384]{1,0:T(8,128)(2,1)S(1)} %get-tuple-element.18), channel_id=1, source_target_pairs={{0,64},{4,68},{64,128},{68,132},{128,192},{132,196},{192,0},{196,4... | collective-permute-start | bytes 589832 | tf_op jit(solution)/shard_map/ppermute | solution.py:263
  71.7 5.5 %collective-permute-start.13 = (bf16[256,384]{1,0:T(8,128)(2,1)S(1)}, bf16[256,384]{1,0:T(8,128)(2,1)S(1)}, u32[]{:S(2)}, u32[]{:S(2)}) collective-permute-start(bf16[256,384]{1,0:T(8,128)(2,1)S(1)} %attend.9), channel_id=1, source_target_pairs={{0,4},{4,0},{64,68},{68,64},{128,132},{132,128},{192,196},{196,192... | collective-permute-start | bytes 589832 | tf_op jit(solution)/shard_map/ppermute | solution.py:263
  74.9 29.1 %copy-start.1 = (bf16[1024,1024]{1,0:T(8,128)(2,1)S(1)}, bf16[1024,1024]{1,0:T(8,128)(2,1)}, u32[]{:S(2)}) copy-start(bf16[1024,1024]{1,0:T(8,128)(2,1)} %w_up_ref.1) | copy-start | bytes 6291460
  74.9 29.1 %copy-start.8 = (bf16[32,1024]{1,0:T(8,128)(2,1)S(1)}, bf16[32,1024]{1,0:T(8,128)(2,1)}, u32[]{:S(2)}) copy-start(bf16[32,1024]{1,0:T(8,128)(2,1)} %latent_ref.3) | copy-start | bytes 196612
  104.0 1.6 %copy-start.2 = (bf16[1024,1024]{1,0:T(8,128)(2,1)S(1)}, bf16[1024,1024]{1,0:T(8,128)(2,1)}, u32[]{:S(2)}) copy-start(bf16[1024,1024]{1,0:T(8,128)(2,1)} %w_down_ref.1) | copy-start | bytes 6291460
  105.6 1.6 %copy-start.3 = (bf16[1024,1024]{1,0:T(8,128)(2,1)S(1)}, bf16[1024,1024]{1,0:T(8,128)(2,1)}, u32[]{:S(2)}) copy-start(bf16[1024,1024]{1,0:T(8,128)(2,1)} %all-gather.3.cloned.1.call-done.w_out_ref) | copy-start | bytes 6291460
  109.2 9.1 %all-to-all-start.2 = ((bf16[4,32,256]{2,1,0:T(8,128)(2,1)}), bf16[4,32,256]{2,1,0:T(8,128)(2,1)S(1)}, u32[]{:S(2)}, u32[]{:S(2)}) async-start(bf16[4,32,256]{2,1,0:T(8,128)(2,1)} %get-tuple-element.24), calls=%async_computation.2 | async-start | bytes 131072 | tf_op jit(solution)/shard_map/all_to_all | solution.py:295
Sparse Core Ops, SparseCore 0:
  9.2 41.8 all-gather.2

commit v2 on v1

--- a/solution.py
+++ b/solution.py
@@ -11,7 +11,8 @@
 HEAD_DIM = 64
 HEADS_HERE = 4
 LANES = 128
-SEQ = ("x", "z", "ylo")
+SEQ = ("xhi", "xlo", "z", "ylo")
+FAR = ("xhi", "z")
 HEAD = ("yhi", "core")
 BF16 = jnp.bfloat16
 F32 = jnp.float32
@@ -35,55 +36,84 @@
     return (widened - row_mean) * lax.rsqrt(row_var + 1e-05)
 
 
-def query_kernel(latent_ref, w_ref, out_ref):
+def query_kernel(latent_hbm, w_hbm, out_ref, latent_ref, w_ref, sems):
+    copies = [
+        pltpu.make_async_copy(latent_hbm, latent_ref, sems.at[0]),
+        pltpu.make_async_copy(w_hbm, w_ref, sems.at[1]),
+    ]
+    for copy in copies:
+        copy.start()
+    copies[0].wait()
     normed = norm_rows(latent_ref[...].astype(F32)).astype(BF16)
+    copies[1].wait()
     out_ref[...] = (product(normed, w_ref[...]) * HEAD_DIM ** (-0.5)).astype(BF16)
 
 
 def make_queries(latent, w_query):
     return pl.pallas_call(
         query_kernel,
+        in_specs=[pl.BlockSpec(memory_space=pltpu.HBM)] * 2,
         out_shape=jax.ShapeDtypeStruct((latent.shape[0], w_query.shape[1]), BF16),
+        scratch_shapes=[
+            pltpu.VMEM(latent.shape, BF16),
+            pltpu.VMEM(w_query.shape, BF16),
+            pltpu.SemaphoreType.DMA((2,)),
+        ],
         compiler_params=params(8),
         name="make_queries",
     )(latent, w_query)
 
 
-def key_value_kernel(x_ref, w_key_ref, w_value_ref, key_ref, value_ref):
-    normed = norm_rows(x_ref[...].astype(F32)).astype(BF16)
-    keys = product(normed, w_key_ref[...]).astype(BF16)
-    vals = product(normed, w_value_ref[...])
-    lane = lax.broadcasted_iota(jnp.int32, (vals.shape[0], LANES), 1)
+def key_value_kernel(
+    block, x_hbm, w_key_hbm, w_value_hbm, key_ref, value_ref, x_ref, w_key_ref, w_value_ref, sems
+):
+    tokens = x_ref.shape[0]
+    weights = [
+        pltpu.make_async_copy(w_key_hbm, w_key_ref, sems.at[0]),
+        pltpu.make_async_copy(w_value_hbm, w_value_ref, sems.at[1]),
+    ]
+    spans = [slice(start, start + block) for start in range(0, tokens, block)]
+    copies = [
+        pltpu.make_async_copy(x_hbm.at[span], x_ref.at[span], sems.at[2 + i])
+        for i, span in enumerate(spans)
+    ]
+    for copy in copies[:1] + weights + copies[1:]:
+        copy.start()
+    lane = lax.broadcasted_iota(jnp.int32, (block, LANES), 1)
     low = lane < HEAD_DIM
-    for head in range(HEADS_HERE):
-        key_ref[head] = keys[:, head * HEAD_DIM : (head + 1) * HEAD_DIM]
-        pair = vals[:, head // 2 * LANES : (head // 2 + 1) * LANES]
-        one = jnp.where(lane == (HEAD_DIM if head % 2 == 0 else 0), 1.0, 0.0)
-        kept = jnp.where(low, pair, one) if head % 2 == 0 else jnp.where(low, one, pair)
-        value_ref[head] = kept.astype(BF16)
+    for i, span in enumerate(spans):
+        copies[i].wait()
+        normed = norm_rows(x_ref[span].astype(F32)).astype(BF16)
+        if i == 0:
+            weights[0].wait()
+            weights[1].wait()
+        keys = product(normed, w_key_ref[...]).astype(BF16)
+        vals = product(normed, w_value_ref[...])
+        for head in range(HEADS_HERE):
+            key_ref[head, span] = keys[:, head * HEAD_DIM : (head + 1) * HEAD_DIM]
+            pair = vals[:, head // 2 * LANES : (head // 2 + 1) * LANES]
+            one = jnp.where(lane == (HEAD_DIM if head % 2 == 0 else 0), 1.0, 0.0)
+            kept = jnp.where(low, pair, one) if head % 2 == 0 else jnp.where(low, one, pair)
+            value_ref[head, span] = kept.astype(BF16)
 
 
 def make_keys_values(x, w_key, w_value):
-    tokens, width = x.shape
+    tokens = x.shape[0]
     block = 512
-    inner = w_key.shape[1]
-    return pl.pallas_call(
-        key_value_kernel,
-        grid=(tokens // block,),
-        in_specs=[
-            pl.BlockSpec((block, width), lambda i: (i, 0)),
-            pl.BlockSpec((width, inner), lambda i: (0, 0)),
-            pl.BlockSpec((width, inner), lambda i: (0, 0)),
-        ],
-        out_specs=[
-            pl.BlockSpec((HEADS_HERE, block, HEAD_DIM), lambda i: (0, i, 0)),
-            pl.BlockSpec((HEADS_HERE, block, LANES), lambda i: (0, i, 0)),
-        ],
+    return pl.pallas_call(
+        functools.partial(key_value_kernel, block),
+        in_specs=[pl.BlockSpec(memory_space=pltpu.HBM)] * 3,
         out_shape=[
             jax.ShapeDtypeStruct((HEADS_HERE, tokens, HEAD_DIM), BF16),
             jax.ShapeDtypeStruct((HEADS_HERE, tokens, LANES), BF16),
         ],
-        compiler_params=params(24),
+        scratch_shapes=[
+            pltpu.VMEM(x.shape, BF16),
+            pltpu.VMEM(w_key.shape, BF16),
+            pltpu.VMEM(w_value.shape, BF16),
+            pltpu.SemaphoreType.DMA((2 + tokens // block,)),
+        ],
+        compiler_params=params(32),
         name="make_keys_values",
     )(x, w_key, w_value)
 
@@ -206,99 +236,98 @@
     )(pieces)
 
 
-def mlp_kernel(att_ref, latent_ref, w_out_ref, w_up_ref, w_down_ref, resid_ref, share_ref):
-    count, _, inner = att_ref.shape
-    projected = latent_ref[...].astype(F32) + functools.reduce(
-        jnp.add,
-        [product(att_ref[i], w_out_ref[i * inner : (i + 1) * inner]) for i in range(count)],
-    )
+def mlp_kernel(one_ref, other_ref, latent_ref, wide_one_ref, wide_other_ref, w_up_ref, w_down_ref, resid_ref, share_ref):
+    count, _, columns = resid_ref.shape
+    projected = latent_ref[...].astype(F32)
+    for att_ref, w_ref in ((one_ref, wide_one_ref), (other_ref, wide_other_ref)):
+        for i in range(att_ref.shape[0]):
+            projected += product(att_ref[i], w_ref[i])
     residual = projected.astype(BF16)
     normed = norm_rows(residual.astype(F32)).astype(BF16)
     raised = product(normed, w_up_ref[...])
     hidden = (0.5 * raised * (1.0 + lax.erf(raised * 0.5**0.5))).astype(BF16)
     share = product(hidden, w_down_ref[...]).astype(BF16)
-    columns = share.shape[1] // count
     for i in range(count):
         resid_ref[i] = residual[:, i * columns : (i + 1) * columns]
         share_ref[i] = share[:, i * columns : (i + 1) * columns]
 
 
-def mlp(att, latent, w_out, w_up, w_down):
-    count, rows, _ = att.shape
+def mlp(one, other, latent, wide_one, wide_other, w_up, w_down):
+    rows = latent.shape[0]
+    count = 2 * one.shape[0]
     out = jax.ShapeDtypeStruct((count, rows, latent.shape[1] // count), BF16)
     return pl.pallas_call(
         mlp_kernel,
         out_shape=[out, out],
         compiler_params=params(24),
         name="mlp",
-    )(att, latent, w_out, w_up, w_down)
-
-
-def close_kernel(place_ref, resid_ref, share_ref, out_ref):
-    total = functools.reduce(jnp.add, [share_ref[i].astype(F32) for i in range(share_ref.shape[0])])
-    out_ref[...] = (resid_ref[place_ref[0]].astype(F32) + total).astype(BF16)
-
-
-def close(place, resid, shares):
+    )(one, other, latent, wide_one, wide_other, w_up, w_down)
+
+
+def close_kernel(place_ref, resid_ref, kept_ref, *refs):
+    out_ref = refs[-1]
+    place = place_ref[0]
+    total = kept_ref[place].astype(F32)
+    for ref in refs[:-1]:
+        total += ref[...].astype(F32)
+    out_ref[...] = (resid_ref[place].astype(F32) + total).astype(BF16)
+
+
+def close(place, resid, kept, *others):
     return pl.pallas_call(
         close_kernel,
-        in_specs=[
-            pl.BlockSpec(memory_space=pltpu.SMEM),
-            pl.BlockSpec(memory_space=pltpu.VMEM),
-            pl.BlockSpec(memory_space=pltpu.VMEM),
-        ],
+        in_specs=[pl.BlockSpec(memory_space=pltpu.SMEM)]
+        + [pl.BlockSpec(memory_space=pltpu.VMEM)] * (2 + len(others)),
         out_shape=jax.ShapeDtypeStruct(resid.shape[1:], BF16),
         compiler_params=params(8),
         name="close",
-    )(place, resid, shares)
-
-
-def moved(value, by_x, by_y):
-    size_x, size_y = lax.axis_size("x"), lax.axis_size("ylo")
-    pairs = []
-    for x in range(size_x):
-        for y in range(size_y):
-            target = (x + by_x) % size_x * size_y + (y + by_y) % size_y
-            pairs.append((x * size_y + y, target))
-    return lax.ppermute(value, ("x", "ylo"), pairs)
-
-
-def along(value, axis, by):
-    size = lax.axis_size(axis)
-    return lax.ppermute(value, axis, [(i, (i + by) % size) for i in range(size)])
+    )(place, resid, kept, *others)
+
+
+def swapped(value, axis):
+    return lax.ppermute(value, axis, [(0, 1), (1, 0)])
+
+
+def crossed(value, by_x, by_y):
+    pairs = [(i, i ^ (by_x * 2 + by_y)) for i in range(4)]
+    return lax.ppermute(value, ("xlo", "ylo"), pairs)
 
 
 def on_device(inputs, latent, w_query, w_key, w_value, w_out, w_up, w_down):
     rows = latent.shape[0]
-    size_z = lax.axis_size("z")
-    w_out_all = lax.all_gather(w_out, HEAD, axis=0, tiled=True)
+    far = lax.axis_size(FAR)
+    wide_one = jnp.stack([w_out, swapped(w_out, "yhi")])
+    wide_other = swapped(wide_one, "core")
     queries = make_queries(latent, w_query)
-    wide = jnp.broadcast_to(queries[None], (size_z,) + queries.shape)
-    column = lax.all_to_all(wide, "z", 0, 0, tiled=True).reshape(size_z * rows, -1)
+    wide = jnp.broadcast_to(queries[None], (far,) + queries.shape)
+    column = lax.all_to_all(wide, FAR, 0, 0, tiled=True).reshape(far * rows, -1)
     keys, values = make_keys_values(inputs, w_key, w_value)
-    shifts = [(1, 0), (3, 0), (2, 0), (2, 1), (1, 1), (3, 1), (0, 1)]
-    arrived = {shift: moved(column, *shift) for shift in shifts}
+    shifts = [(0, 1), (1, 1), (1, 0)]
+    arrived = [crossed(column, *shift) for shift in shifts]
     pieces = []
-    groups = [[None], shifts[0:2], shifts[2:4], shifts[4:6], shifts[6:7]]
-    for group in groups:
-        chunks = [column if shift is None else arrived[shift] for shift in group]
-        outs = attend(chunks, keys, values)
-        for shift, out in zip(group, outs):
-            if shift is not None:
-                out = moved(out, -shift[0], -shift[1])
-            pieces.append(out)
+    for shift, chunk in zip(shifts, arrived):
+        pieces.append(crossed(attend([chunk], keys, values)[0], *shift))
+    pieces.append(attend([column], keys, values)[0])
     block = merge(pieces)
-    parts = lax.all_to_all(block.reshape(size_z, rows, -1), "z", 0, 0, tiled=True)
+    parts = lax.all_to_all(block.reshape(far, rows, -1), FAR, 0, 0, tiled=True)
     attended = finish(parts)
-    att = lax.all_gather(attended, HEAD, axis=0)
-    resid, shares = mlp(att, latent, w_out_all, w_up, w_down)
-    shares = lax.all_to_all(shares, HEAD, 0, 0, tiled=True)
-    place = lax.axis_index(HEAD).astype(jnp.int32).reshape(1)
-    return close(place, resid, shares)
+    att_one = jnp.stack([attended, swapped(attended, "yhi")])
+    att_other = swapped(att_one, "core")
+    resid, shares = mlp(att_one, att_other, latent, wide_one, wide_other, w_up, w_down)
+    yhi, core = lax.axis_index("yhi"), lax.axis_index("core")
+
+    def block_of(high, low):
+        return lax.dynamic_index_in_dim(shares, high * 2 + low, 0, keepdims=False)
+
+    by_core = swapped(block_of(yhi, 1 - core), "core")
+    by_high = swapped(block_of(1 - yhi, core), "yhi")
+    by_both = lax.ppermute(block_of(1 - yhi, 1 - core), HEAD, [(i, 3 - i) for i in range(4)])
+    place = (yhi * 2 + core).astype(jnp.int32).reshape(1)
+    return close(place, resid, shares, by_core, by_high, by_both)
 
 
 def solution(mesh):
-    fine = Mesh(mesh.devices.reshape(4, 8, 2, 2, 2), SEQ + HEAD)
+    fine = Mesh(mesh.devices.reshape(2, 2, 8, 2, 2, 2), SEQ + HEAD)
     placed = (
         P(SEQ, None),
         P(SEQ, None),

time: 126 us -> 112 us (0.89)
  blocking collectives: 42.1 us -> 17.7 us
  between operations: 13.6 us -> 0.15 us
  starting transfers between devices: 23.2 us -> 34.8 us
  waiting for transfers between devices: 7.83 us -> 19.4 us
    all_gather x1 -> x0, blocking collectives: 14.5 us -> none  [on_device(): att = lax.all_gather(attended, HEAD, axis=0)]
    all_to_all x2 -> x1, blocking collectives: 27.6 us -> 17.7 us  [on_device(): parts = lax.all_to_all(block.reshape(far, rows, -1), FAR, 0, 0, tiled=True)]
    ppermute x14 -> x13, waiting for transfers between devices: 2.35 us -> 12.2 us  [the longest x6 5.78 us: crossed(): return lax.ppermute(value, ('xlo', 'ylo'), pairs)]
    all_to_all x1, starting transfers between devices: 4.35 us -> 11.6 us  [on_device(): column = lax.all_to_all(wide, FAR, 0, 0, tiled=True).reshape(far * rows, -1)]
    ppermute x14 -> x13, starting transfers between devices: 18.9 us -> 23.3 us  [the longest x6 16.8 us: swapped(): return lax.ppermute(value, axis, [(0, 1), (1, 0)])]
    all_to_all x1, waiting for transfers between devices: 4.76 us -> 7.23 us  [on_device(): column = lax.all_to_all(wide, FAR, 0, 0, tiled=True).reshape(far * rows, -1)]
    unnamed x18, local copies, waits for them, and re-layouts: 9.33 us -> 7.76 us
    pallas_call x5 -> x4, Pallas kernels: 21.4 us -> 21 us  [attend(): pl.pallas_call(functools.partial(attend_kernel, count), out_shape=[jax.Sh...]
  transfers between devices with their start and end apart: 16 -> 14, of which waited for: 2 -> 6; matrix products, arithmetic and copies ran while one was open for 0% -> 0% of each run, Pallas kernels for 22% -> 24%
where the time goes in v2:
time: 112 us; the launch traced here: 111 us
  starting transfers between devices  34.8 us (31%)
  Pallas kernels  30.8 us (28%)
  waiting for transfers between devices  19.4 us (17%)
  blocking collectives  17.7 us (16%)
  local copies, waits for them, and re-layouts  8.5 us (8%)
    pallas_call x4, Pallas kernels, attend(): pl.pallas_call(functools.partial(attend_kernel, count), out_shape=[jax.Sh...  21 us
    all_to_all x1, blocking collectives, on_device(): parts = lax.all_to_all(block.reshape(far, rows, -1), FAR, 0, 0, tiled=True)  17.7 us
    ppermute x6, starting transfers between devices, swapped(): return lax.ppermute(value, axis, [(0, 1), (1, 0)])  16.8 us
    all_to_all x1, starting transfers between devices, on_device(): column = lax.all_to_all(wide, FAR, 0, 0, tiled=True).reshape(far * rows, -1)  11.6 us
    unnamed x18, local copies, waits for them, and re-layouts  7.76 us
    all_to_all x1, waiting for transfers between devices, on_device(): column = lax.all_to_all(wide, FAR, 0, 0, tiled=True).reshape(far * rows, -1)  7.23 us
    ppermute x6, starting transfers between devices, crossed(): return lax.ppermute(value, ('xlo', 'ylo'), pairs)  5.79 us
    ppermute x6, waiting for transfers between devices, crossed(): return lax.ppermute(value, ('xlo', 'ylo'), pairs)  5.78 us
  transfers between devices with their start and end apart: 14, of which 6 were waited for; matrix products, arithmetic and copies ran while one was open for 0% of the time, Pallas kernels for 24%

profile of v2, /device:TPU:1, one launch (start us, length us, event | category | flops | bytes accessed | tf_op | source)
XLA Modules:
  0.0 111.4 jit_solution(18192903355250354346)
XLA Ops:
  0.0 1.0 copy-done.5
  1.0 0.8 copy-done.6
  2.3 0.7 broadcast_in_dim.2
  3.0 11.6 %all-to-all-start = ((bf16[16,32,256]{2,1,0:T(8,128)(2,1)}), bf16[16,32,256]{2,1,0:T(8,128)(2,1)S(1)}, u32[]{:S(2)}, u32[]{:S(2)}) async-start(bf16[16,32,256]{2,1,0:T(8,128)(2,1)} %broadcast_in_dim.2), calls=%async_computation | async-start | bytes 524288 | tf_op jit(solution)/shard_map/all_to_all | solution.py:303
  14.6 3.0 %collective-permute-start.8 = (bf16[256,1024]{1,0:T(8,128)(2,1)}, bf16[256,1024]{1,0:T(8,128)(2,1)S(1)}, u32[]{:S(2)}, u32[]{:S(2)}) collective-permute-start(bf16[256,1024]{1,0:T(8,128)(2,1)} %param.13), channel_id=1, source_target_pairs={{0,2},{2,0},{1,3},{3,1},{4,6},{6,4},{5,7},{7,5},{8,10},{10,8},{9,1... | collective-permute-start | bytes 1572872 | tf_op jit(solution)/shard_map/ppermute | solution.py:288
  17.6 7.2 %all-to-all-done = bf16[16,32,256]{2,1,0:T(8,128)(2,1)S(1)} async-done(((bf16[16,32,256]{2,1,0:T(8,128)(2,1)}), bf16[16,32,256]{2,1,0:T(8,128)(2,1)S(1)}, u32[]{:S(2)}, u32[]{:S(2)}) %all-to-all-start) | async-done | bytes 262176 | tf_op jit(solution)/shard_map/all_to_all | solution.py:303
  25.2 2.2 %collective-permute-start.2 = (bf16[512,256]{1,0:T(8,128)(2,1)S(1)}, bf16[512,256]{1,0:T(8,128)(2,1)S(1)}, u32[]{:S(2)}, u32[]{:S(2)}) collective-permute-start(bf16[512,256]{1,0:T(8,128)(2,1)S(1)} %bitcast.15), channel_id=1, source_target_pairs={{0,68},{4,64},{64,4},{68,0},{1,69},{5,65},{65,5},{69,1},{2,70},{6,... | collective-permute-start | bytes 786440 | tf_op jit(solution)/shard_map/ppermute | solution.py:293
  27.5 2.2 %copy-done = bf16[2048,1024]{1,0:T(8,128)(2,1)S(1)} copy-done((bf16[2048,1024]{1,0:T(8,128)(2,1)S(1)}, bf16[2048,1024]{1,0:T(8,128)(2,1)}, u32[]{:S(2)}) %copy-start) | copy-done | bytes 4194328
  29.7 1.0 copy-done.3
  30.7 1.0 copy-done.4
  31.8 4.8 %make_keys_values.1 = (bf16[4,2048,64]{2,1,0:T(8,128)(2,1)S(1)}, bf16[4,2048,128]{2,1,0:T(8,128)(2,1)S(1)}) custom-call(bf16[2048,1024]{1,0:T(8,128)(2,1)S(1)} %copy-done, bf16[1024,256]{1,0:T(8,128)(2,1)S(1)} %copy-done.3, bf16[1024,256]{1,0:T(8,128)(2,1)S(1)} %copy-done.4), custom_call_target="tpu_custom_call" | custom-call | tf_op jit(solution)/shard_map/make_keys_values/pallas_call | solution.py:103
  36.6 5.3 %attend.6 = bf16[512,384]{1,0:T(8,128)(2,1)S(1)} custom-call(bf16[512,256]{1,0:T(8,128)(2,1)S(1)} %collective-permute-done.4.refs_0_, bf16[4,2048,64]{2,1,0:T(8,128)(2,1)S(1)} %get-tuple-element.9.refs_1_, bf16[4,2048,128]{2,1,0:T(8,128)(2,1)S(1)} %get-tuple-element.10.refs_2_), custom_call_target="tpu_custom_call" | custom-call | tf_op jit(solution)/shard_map/attend/pallas_call | solution.py:172
  41.9 0.6 collective-permute-start.5
  42.5 5.2 %attend.5 = bf16[512,384]{1,0:T(8,128)(2,1)S(1)} custom-call(bf16[512,256]{1,0:T(8,128)(2,1)S(1)} %collective-permute-done.2.refs_0_, bf16[4,2048,64]{2,1,0:T(8,128)(2,1)S(1)} %get-tuple-element.9.refs_1_, bf16[4,2048,128]{2,1,0:T(8,128)(2,1)S(1)} %get-tuple-element.10.refs_2_), custom_call_target="tpu_custom_call" | custom-call | tf_op jit(solution)/shard_map/attend/pallas_call | solution.py:172
  47.8 2.3 %collective-permute-start.3 = (bf16[512,384]{1,0:T(8,128)(2,1)S(1)}, bf16[512,384]{1,0:T(8,128)(2,1)S(1)}, u32[]{:S(2)}, u32[]{:S(2)}) collective-permute-start(bf16[512,384]{1,0:T(8,128)(2,1)S(1)} %attend.5), channel_id=1, source_target_pairs={{0,68},{4,64},{64,4},{68,0},{1,69},{5,65},{65,5},{69,1},{2,70},{6,... | collective-permute-start | bytes 1179656 | tf_op jit(solution)/shard_map/ppermute | solution.py:293
  50.0 5.2 %attend.4 = bf16[512,384]{1,0:T(8,128)(2,1)S(1)} custom-call(bf16[512,256]{1,0:T(8,128)(2,1)S(1)} %collective-permute-done.refs_0_, bf16[4,2048,64]{2,1,0:T(8,128)(2,1)S(1)} %get-tuple-element.9.refs_1_, bf16[4,2048,128]{2,1,0:T(8,128)(2,1)S(1)} %get-tuple-element.10.refs_2_), custom_call_target="tpu_custom_call" | custom-call | tf_op jit(solution)/shard_map/attend/pallas_call | solution.py:172
  55.6 4.4 %collective-permute-start.9 = (bf16[2,256,1024]{2,1,0:T(8,128)(2,1)S(1)}, bf16[2,256,1024]{2,1,0:T(8,128)(2,1)}, u32[]{:S(2)}, u32[]{:S(2)}) collective-permute-start(bf16[2,256,1024]{2,1,0:T(8,128)(2,1)S(1)} %pad_maximum_fusion.wide_one_ref), channel_id=1, source_target_pairs={{0,1},{1,0},{2,3},{3,2},{4,5},{5,4},{6,7},{7,6},{8,9},{9,8},{10,11... | collective-permute-start | bytes 3145736 | tf_op jit(solution)/shard_map/ppermute | solution.py:288
  60.0 5.3 %attend.7.refs_3_ = bf16[512,384]{1,0:T(8,128)(2,1)S(1)} custom-call(bf16[512,256]{1,0:T(8,128)(2,1)S(1)} %bitcast.17, bf16[4,2048,64]{2,1,0:T(8,128)(2,1)S(1)} %get-tuple-element.9.refs_1_, bf16[4,2048,128]{2,1,0:T(8,128)(2,1)S(1)} %get-tuple-element.10.refs_2_), custom_call_target="tpu_custom_call" | custom-call | tf_op jit(solution)/shard_map/attend/pallas_call | solution.py:172
  65.3 5.8 %collective-permute-done.1.refs_0_ = bf16[512,384]{1,0:T(8,128)(2,1)S(1)} collective-permute-done((bf16[512,384]{1,0:T(8,128)(2,1)S(1)}, bf16[512,384]{1,0:T(8,128)(2,1)S(1)}, u32[]{:S(2)}, u32[]{:S(2)}) %collective-permute-start.1) | collective-permute-done | bytes 393248 | tf_op jit(solution)/shard_map/ppermute | solution.py:293
  71.1 1.0 merge.1
  72.1 17.7 %all_to_all.10.pieces_ref = bf16[16,32,384]{2,1,0:T(8,128)(2,1)S(1)} all-to-all(bf16[16,32,384]{2,1,0:T(8,128)(2,1)S(1)} %bitcast.13), channel_id=1, replica_groups=mesh['xhi'=2,'xlo'=2,'z'=8,'ylo'=2,'yhi'=2,'core'=2] {'xhi','z'}, dimensions={0} | all-to-all | bytes 786432 | tf_op jit(solution)/shard_map/all_to_all | solution.py:312
  90.1 2.7 %collective-permute-start.6 = (bf16[32,256]{1,0:T(8,128)(2,1)S(1)}, bf16[32,256]{1,0:T(8,128)(2,1)S(1)}, u32[]{:S(2)}, u32[]{:S(2)}) collective-permute-start(bf16[32,256]{1,0:T(8,128)(2,1)S(1)} %finish.1), channel_id=1, source_target_pairs={{0,2},{2,0},{1,3},{3,1},{4,6},{6,4},{5,7},{7,5},{8,10},{10,8},{9,1... | collective-permute-start | bytes 49160 | tf_op jit(solution)/shard_map/ppermute | solution.py:288
  92.8 1.5 %collective-permute-done.6 = bf16[32,256]{1,0:T(8,128)(2,1)S(1)} collective-permute-done((bf16[32,256]{1,0:T(8,128)(2,1)S(1)}, bf16[32,256]{1,0:T(8,128)(2,1)S(1)}, u32[]{:S(2)}, u32[]{:S(2)}) %collective-permute-start.6) | collective-permute-done | bytes 16416 | tf_op jit(solution)/shard_map/ppermute | solution.py:288
  94.2 3.7 %collective-permute-start.7 = (bf16[2,32,256]{2,1,0:T(8,128)(2,1)S(1)}, bf16[2,32,256]{2,1,0:T(8,128)(2,1)S(1)}, u32[]{:S(2)}, u32[]{:S(2)}) collective-permute-start(bf16[2,32,256]{2,1,0:T(8,128)(2,1)S(1)} %pad_maximum_fusion.1.one_ref), channel_id=1, source_target_pairs={{0,1},{1,0},{2,3},{3,2},{4,5},{5,4},{6,7},{7,6},{8,9},{9,8},{10,11... | collective-permute-start | bytes 98312 | tf_op jit(solution)/shard_map/ppermute | solution.py:288
  97.9 0.9 collective-permute-done.7.other_ref
  98.8 1.6 %copy-done.2 = bf16[1024,1024]{1,0:T(8,128)(2,1)S(1)} copy-done((bf16[1024,1024]{1,0:T(8,128)(2,1)S(1)}, bf16[1024,1024]{1,0:T(8,128)(2,1)}, u32[]{:S(2)}) %copy-start.2) | copy-done | bytes 2097176
  100.4 2.6 %mlp.1 = (bf16[4,32,256]{2,1,0:T(8,128)(2,1)S(1)}, bf16[4,32,256]{2,1,0:T(8,128)(2,1)S(1)}) custom-call(bf16[2,32,256]{2,1,0:T(8,128)(2,1)S(1)} %pad_maximum_fusion.1.one_ref, bf16[2,32,256]{2,1,0:T(8,128)(2,1)S(1)} %collective-permute-done.7.other_ref, bf16[32,1024]{1,0:T(8,128)(2,1)S(1)} %copy-done.7, ...), custom_call_target="tpu_custom_call" | custom-call | tf_op jit(solution)/shard_map/mlp/pallas_call | solution.py:259
  103.4 2.7 %collective-permute-start.11 = (bf16[32,256]{1,0:T(8,128)(2,1)S(1)}, bf16[32,256]{1,0:T(8,128)(2,1)S(1)}, u32[]{:S(2)}, u32[]{:S(2)}) collective-permute-start(bf16[32,256]{1,0:T(8,128)(2,1)S(1)} %get-tuple-element.14), channel_id=1, source_target_pairs={{0,2},{2,0},{1,3},{3,1},{4,6},{6,4},{5,7},{7,5},{8,10},{10,8},{9,1... | collective-permute-start | bytes 49160 | tf_op jit(solution)/shard_map/ppermute | solution.py:288
  106.1 0.6 collective-permute-start.12
  106.7 0.8 collective-permute-done.11.refs_1_
  107.5 3.3 %collective-permute-done.12.refs_2_ = bf16[32,256]{1,0:T(8,128)(2,1)S(1)} collective-permute-done((bf16[32,256]{1,0:T(8,128)(2,1)S(1)}, bf16[32,256]{1,0:T(8,128)(2,1)S(1)}, u32[]{:S(2)}, u32[]{:S(2)}) %collective-permute-start.12) | collective-permute-done | bytes 16416 | tf_op jit(solution)/shard_map/ppermute | solution.py:324
  110.8 0.6 close.1
  (29 shorter events, 2.1 us)
Async XLA Ops:
  0.0 1.0 copy-start.5
  1.0 0.8 copy-start.6
  3.0 21.8 %all-to-all-start = ((bf16[16,32,256]{2,1,0:T(8,128)(2,1)}), bf16[16,32,256]{2,1,0:T(8,128)(2,1)S(1)}, u32[]{:S(2)}, u32[]{:S(2)}) async-start(bf16[16,32,256]{2,1,0:T(8,128)(2,1)} %broadcast_in_dim.2), calls=%async_computation | async-start | bytes 524288 | tf_op jit(solution)/shard_map/all_to_all | solution.py:303
  14.6 40.9 %collective-permute-start.8 = (bf16[256,1024]{1,0:T(8,128)(2,1)}, bf16[256,1024]{1,0:T(8,128)(2,1)S(1)}, u32[]{:S(2)}, u32[]{:S(2)}) collective-permute-start(bf16[256,1024]{1,0:T(8,128)(2,1)} %param.13), channel_id=1, source_target_pairs={{0,2},{2,0},{1,3},{3,1},{4,6},{6,4},{5,7},{7,5},{8,10},{10,8},{9,1... | collective-permute-start | bytes 1572872 | tf_op jit(solution)/shard_map/ppermute | solution.py:288
  24.9 11.7 %collective-permute-start.4 = (bf16[512,256]{1,0:T(8,128)(2,1)S(1)}, bf16[512,256]{1,0:T(8,128)(2,1)S(1)}, u32[]{:S(2)}, u32[]{:S(2)}) collective-permute-start(bf16[512,256]{1,0:T(8,128)(2,1)S(1)} %bitcast.14), channel_id=1, source_target_pairs={{0,64},{4,68},{64,0},{68,4},{1,65},{5,69},{65,1},{69,5},{2,66},{6,... | collective-permute-start | bytes 786440 | tf_op jit(solution)/shard_map/ppermute | solution.py:293
  25.2 17.3 %collective-permute-start.2 = (bf16[512,256]{1,0:T(8,128)(2,1)S(1)}, bf16[512,256]{1,0:T(8,128)(2,1)S(1)}, u32[]{:S(2)}, u32[]{:S(2)}) collective-permute-start(bf16[512,256]{1,0:T(8,128)(2,1)S(1)} %bitcast.15), channel_id=1, source_target_pairs={{0,68},{4,64},{64,4},{68,0},{1,69},{5,65},{65,5},{69,1},{2,70},{6,... | collective-permute-start | bytes 786440 | tf_op jit(solution)/shard_map/ppermute | solution.py:293
  27.3 22.7 %collective-permute-start = (bf16[512,256]{1,0:T(8,128)(2,1)S(1)}, bf16[512,256]{1,0:T(8,128)(2,1)S(1)}, u32[]{:S(2)}, u32[]{:S(2)}) collective-permute-start(bf16[512,256]{1,0:T(8,128)(2,1)S(1)} %bitcast.16), channel_id=1, source_target_pairs={{0,4},{4,0},{64,68},{68,64},{1,5},{5,1},{65,69},{69,65},{2,6},{6,2... | collective-permute-start | bytes 786440 | tf_op jit(solution)/shard_map/ppermute | solution.py:293
  27.5 2.2 %copy-start = (bf16[2048,1024]{1,0:T(8,128)(2,1)S(1)}, bf16[2048,1024]{1,0:T(8,128)(2,1)}, u32[]{:S(2)}) copy-start(bf16[2048,1024]{1,0:T(8,128)(2,1)} %x_hbm.1) | copy-start | bytes 12582916
  29.7 1.0 copy-start.3
  30.7 1.0 copy-start.4
  41.9 23.4 %collective-permute-start.5 = (bf16[512,384]{1,0:T(8,128)(2,1)S(1)}, bf16[512,384]{1,0:T(8,128)(2,1)S(1)}, u32[]{:S(2)}, u32[]{:S(2)}) collective-permute-start(bf16[512,384]{1,0:T(8,128)(2,1)S(1)} %attend.6), channel_id=1, source_target_pairs={{0,64},{4,68},{64,0},{68,4},{1,65},{5,69},{65,1},{69,5},{2,66},{6,... | collective-permute-start | bytes 1179656 | tf_op jit(solution)/shard_map/ppermute | solution.py:293
  47.7 7.8 %copy-start.8 = (bf16[256,1024]{1,0:T(8,128)(2,1)S(1)}, bf16[256,1024]{1,0:T(8,128)(2,1)}, u32[]{:S(2)}) copy-start(bf16[256,1024]{1,0:T(8,128)(2,1)} %param.13) | copy-start | bytes 1572868
  47.8 17.5 %collective-permute-start.3 = (bf16[512,384]{1,0:T(8,128)(2,1)S(1)}, bf16[512,384]{1,0:T(8,128)(2,1)S(1)}, u32[]{:S(2)}, u32[]{:S(2)}) collective-permute-start(bf16[512,384]{1,0:T(8,128)(2,1)S(1)} %attend.5), channel_id=1, source_target_pairs={{0,68},{4,64},{64,4},{68,0},{1,69},{5,65},{65,5},{69,1},{2,70},{6,... | collective-permute-start | bytes 1179656 | tf_op jit(solution)/shard_map/ppermute | solution.py:293
  55.3 15.8 %collective-permute-start.1 = (bf16[512,384]{1,0:T(8,128)(2,1)S(1)}, bf16[512,384]{1,0:T(8,128)(2,1)S(1)}, u32[]{:S(2)}, u32[]{:S(2)}) collective-permute-start(bf16[512,384]{1,0:T(8,128)(2,1)S(1)} %attend.4), channel_id=1, source_target_pairs={{0,4},{4,0},{64,68},{68,64},{1,5},{5,1},{65,69},{69,65},{2,6},{6,2... | collective-permute-start | bytes 1179656 | tf_op jit(solution)/shard_map/ppermute | solution.py:293
  55.6 42.3 %collective-permute-start.9 = (bf16[2,256,1024]{2,1,0:T(8,128)(2,1)S(1)}, bf16[2,256,1024]{2,1,0:T(8,128)(2,1)}, u32[]{:S(2)}, u32[]{:S(2)}) collective-permute-start(bf16[2,256,1024]{2,1,0:T(8,128)(2,1)S(1)} %pad_maximum_fusion.wide_one_ref), channel_id=1, source_target_pairs={{0,1},{1,0},{2,3},{3,2},{4,5},{5,4},{6,7},{7,6},{8,9},{9,8},{10,11... | collective-permute-start | bytes 3145736 | tf_op jit(solution)/shard_map/ppermute | solution.py:288
  65.3 33.5 %copy-start.1 = (bf16[1024,1024]{1,0:T(8,128)(2,1)S(1)}, bf16[1024,1024]{1,0:T(8,128)(2,1)}, u32[]{:S(2)}) copy-start(bf16[1024,1024]{1,0:T(8,128)(2,1)} %w_up_ref.1) | copy-start | bytes 6291460
  65.3 33.5 %copy-start.7 = (bf16[32,1024]{1,0:T(8,128)(2,1)S(1)}, bf16[32,1024]{1,0:T(8,128)(2,1)}, u32[]{:S(2)}) copy-start(bf16[32,1024]{1,0:T(8,128)(2,1)} %latent_ref.1) | copy-start | bytes 196612
  90.1 4.2 %collective-permute-start.6 = (bf16[32,256]{1,0:T(8,128)(2,1)S(1)}, bf16[32,256]{1,0:T(8,128)(2,1)S(1)}, u32[]{:S(2)}, u32[]{:S(2)}) collective-permute-start(bf16[32,256]{1,0:T(8,128)(2,1)S(1)} %finish.1), channel_id=1, source_target_pairs={{0,2},{2,0},{1,3},{3,1},{4,6},{6,4},{5,7},{7,5},{8,10},{10,8},{9,1... | collective-permute-start | bytes 49160 | tf_op jit(solution)/shard_map/ppermute | solution.py:288
  94.2 4.5 %collective-permute-start.7 = (bf16[2,32,256]{2,1,0:T(8,128)(2,1)S(1)}, bf16[2,32,256]{2,1,0:T(8,128)(2,1)S(1)}, u32[]{:S(2)}, u32[]{:S(2)}) collective-permute-start(bf16[2,32,256]{2,1,0:T(8,128)(2,1)S(1)} %pad_maximum_fusion.1.one_ref), channel_id=1, source_target_pairs={{0,1},{1,0},{2,3},{3,2},{4,5},{5,4},{6,7},{7,6},{8,9},{9,8},{10,11... | collective-permute-start | bytes 98312 | tf_op jit(solution)/shard_map/ppermute | solution.py:288
  98.8 1.6 %copy-start.2 = (bf16[1024,1024]{1,0:T(8,128)(2,1)S(1)}, bf16[1024,1024]{1,0:T(8,128)(2,1)}, u32[]{:S(2)}) copy-start(bf16[1024,1024]{1,0:T(8,128)(2,1)} %w_down_ref.1) | copy-start | bytes 6291460
  103.0 3.7 %collective-permute-start.10 = (bf16[32,256]{1,0:T(8,128)(2,1)S(1)}, bf16[32,256]{1,0:T(8,128)(2,1)S(1)}, u32[]{:S(2)}, u32[]{:S(2)}) collective-permute-start(bf16[32,256]{1,0:T(8,128)(2,1)S(1)} %get-tuple-element.15), channel_id=1, source_target_pairs={{0,1},{1,0},{2,3},{3,2},{4,5},{5,4},{6,7},{7,6},{8,9},{9,8},{10,11... | collective-permute-start | bytes 49160 | tf_op jit(solution)/shard_map/ppermute | solution.py:288
  103.4 4.1 %collective-permute-start.11 = (bf16[32,256]{1,0:T(8,128)(2,1)S(1)}, bf16[32,256]{1,0:T(8,128)(2,1)S(1)}, u32[]{:S(2)}, u32[]{:S(2)}) collective-permute-start(bf16[32,256]{1,0:T(8,128)(2,1)S(1)} %get-tuple-element.14), channel_id=1, source_target_pairs={{0,2},{2,0},{1,3},{3,1},{4,6},{6,4},{5,7},{7,5},{8,10},{10,8},{9,1... | collective-permute-start | bytes 49160 | tf_op jit(solution)/shard_map/ppermute | solution.py:288
  106.1 4.7 %collective-permute-start.12 = (bf16[32,256]{1,0:T(8,128)(2,1)S(1)}, bf16[32,256]{1,0:T(8,128)(2,1)S(1)}, u32[]{:S(2)}, u32[]{:S(2)}) collective-permute-start(bf16[32,256]{1,0:T(8,128)(2,1)S(1)} %get-tuple-element.13), channel_id=1, source_target_pairs={{0,3},{1,2},{2,1},{3,0},{4,7},{5,6},{6,5},{7,4},{8,11},{9,10},{10,... | collective-permute-start | bytes 49160 | tf_op jit(solution)/shard_map/ppermute | solution.py:324
